TPU v7x, 32 devices: a whole 2x2x4 slice. The times are simulated.
32 devices in a mesh: dp: 8 (over z, x), tensor: 4 (over y, core).
Axes of the slice: x: 2, y: 2, z: 4, core: 2. Of those that a mesh axis runs over, the one named last changes fastest.
Arguments:
- layer_input: float32 [8, 1024, 768], P('dp', 'tensor'), may hold values from -40 to 40
- out_cotangent: float32 [8, 1024, 768], P('dp', 'tensor'), may hold values from -6 to 6
- mix_gain: bfloat16 [768], P('dp'), may hold values from 0.099609375 to 1.8984375
- mix_shift: bfloat16 [768], P('dp'), may hold values from -4 to 4
- query_weight: bfloat16 [768, 768], P('dp', 'tensor'), may hold values from -2 to 2
- query_bias: bfloat16 [64, 12], P('dp', 'tensor'), may hold values from -3 to 3
- key_weight: bfloat16 [768, 768], P('dp', 'tensor'), may hold values from -2 to 2
- value_weight: bfloat16 [768, 768], P('dp', 'tensor'), may hold values from -0.21875 to 0.21875
- value_bias: bfloat16 [64, 12], P('dp', 'tensor'), may hold values from -0.59765625 to 0.59765625
- output_weight: bfloat16 [768, 768], P('dp', 'tensor'), may hold values from -1.75 to 1.75
- output_bias: bfloat16 [768], P('dp'), may hold values from -4 to 4
- feed_gain: bfloat16 [768], P('dp'), may hold values from 0.099609375 to 1.8984375
- feed_shift: bfloat16 [768], P('dp'), may hold values from -4 to 4
- inner_weight: bfloat16 [768, 3072], P('dp', 'tensor'), may hold values from -0.21875 to 0.21875
- inner_bias: bfloat16 [64, 48], P('dp', 'tensor'), may hold values from -3 to 3
- outer_weight: bfloat16 [768, 3072], P('dp', 'tensor'), may hold values from -0.3125 to 0.3125
- outer_bias: bfloat16 [768], P('dp'), may hold values from -4 to 4
Outputs:
- layer_output: float32 [8, 1024, 768], P('dp', 'tensor')
- input_grad: float32 [8, 1024, 768], P('dp', 'tensor')
- mix_gain_grad: float32 [768], P(('dp', 'tensor'))
- mix_shift_grad: float32 [768], P(('dp', 'tensor'))
- query_weight_grad: float32 [768, 768], P('dp', 'tensor')
- query_bias_grad: float32 [64, 12], P('dp', 'tensor')
- key_weight_grad: float32 [768, 768], P('dp', 'tensor')
- value_weight_grad: float32 [768, 768], P('dp', 'tensor')
- value_bias_grad: float32 [64, 12], P('dp', 'tensor')
- output_weight_grad: float32 [768, 768], P('dp', 'tensor')
- output_bias_grad: float32 [768], P(('dp', 'tensor'))
- feed_gain_grad: float32 [768], P(('dp', 'tensor'))
- feed_shift_grad: float32 [768], P(('dp', 'tensor'))
- inner_weight_grad: float32 [768, 3072], P('dp', 'tensor')
- inner_bias_grad: float32 [64, 48], P('dp', 'tensor')
- outer_weight_grad: float32 [768, 3072], P('dp', 'tensor')
- outer_bias_grad: float32 [768], P(('dp', 'tensor'))
All inputs are finite; a program needn't handle non-finite values.
Results may differ from a plain program's by a relative error of at most 0.02.
Values may be sent and summed in bfloat16 or wider, within the bound.
A program may use at most 128 MiB of HBM per device.

v0:
```python
import math
import jax
import jax.numpy as jnp
from jax import lax
from jax.sharding import PartitionSpec as P

HD = 64
EPS = 1e-05
ROOT_HALF = 0.7071067811865476
DENSITY_NORM = 0.3989422804014327


def layer_norm(block, gain, shift):
    row_mean = jnp.mean(block, axis=-1, keepdims=True)
    centred = block - row_mean
    rstd = lax.rsqrt(jnp.mean(centred * centred, axis=-1, keepdims=True) + EPS)
    normed = centred * rstd
    lowered = (normed * gain.astype(jnp.float32) + shift.astype(jnp.float32)).astype(jnp.bfloat16)
    return (normed, rstd, lowered)


def norm_backward(gradient, normed, rstd, gain):
    scaled = gradient * gain.astype(jnp.float32)
    first = jnp.mean(scaled, axis=-1, keepdims=True)
    second = jnp.mean(scaled * normed, axis=-1, keepdims=True)
    return (scaled - first - normed * second) * rstd


def gelu_value(preact):
    return 0.5 * preact * (1.0 + lax.erf(preact * ROOT_HALF))


def gelu_slope(preact):
    return 0.5 * (1.0 + lax.erf(preact * ROOT_HALF)) + preact * DENSITY_NORM * jnp.exp(
        -0.5 * preact * preact
    )


def matmul(left, right):
    return jnp.dot(left, right, preferred_element_type=jnp.float32)


def token_product(left, right):
    return lax.dot_general(
        left, right, (((0,), (0,)), ((), ())), preferred_element_type=jnp.float32
    )


def split_heads(block):
    return block.reshape(block.shape[0], block.shape[1] // HD, HD)


def attend(operands):
    queries, key_rows, values = operands
    score_scale = 1.0 / math.sqrt(HD)
    scores = (
        jnp.einsum(
            "qhd,khd->hqk",
            split_heads(queries),
            split_heads(key_rows),
            preferred_element_type=jnp.float32,
        )
        * score_scale
    )
    row_max = jnp.max(scores, axis=-1, keepdims=True)
    log_total = row_max + jnp.log(jnp.sum(jnp.exp(scores - row_max), axis=-1, keepdims=True))
    prob_low = jnp.exp(scores - log_total).astype(jnp.bfloat16)
    context = jnp.einsum(
        "hqk,khd->qhd", prob_low, split_heads(values), preferred_element_type=jnp.float32
    )
    return (context.reshape(queries.shape).astype(jnp.bfloat16), log_total)


def attend_back(operands):
    queries, key_rows, values, context_grad, log_total = operands
    score_scale = 1.0 / math.sqrt(HD)
    query_heads = split_heads(queries)
    key_heads = split_heads(key_rows)
    grad_heads = split_heads(context_grad)
    scores = (
        jnp.einsum("qhd,khd->hqk", query_heads, key_heads, preferred_element_type=jnp.float32)
        * score_scale
    )
    prob_full = jnp.exp(scores - log_total)
    prob_low = prob_full.astype(jnp.bfloat16)
    value_grad = jnp.einsum(
        "hqk,qhd->khd", prob_low, grad_heads, preferred_element_type=jnp.float32
    )
    prob_grad = jnp.einsum(
        "qhd,khd->hqk", grad_heads, split_heads(values), preferred_element_type=jnp.float32
    )
    row_dot = jnp.sum(prob_full * prob_grad, axis=-1, keepdims=True)
    score_grad = (prob_full * (prob_grad - row_dot) * score_scale).astype(jnp.bfloat16)
    query_grad = jnp.einsum(
        "hqk,khd->qhd", score_grad, key_heads, preferred_element_type=jnp.float32
    )
    key_low = jnp.einsum(
        "hqk,qhd->khd", score_grad, query_heads, preferred_element_type=jnp.float32
    ).astype(jnp.bfloat16)
    return (
        query_grad.reshape(queries.shape),
        key_low.reshape(queries.shape),
        value_grad.reshape(queries.shape),
    )


def on_device(
    layer_input,
    out_cotangent,
    mix_gain,
    mix_shift,
    query_weight,
    query_bias,
    key_weight,
    value_weight,
    value_bias,
    output_weight,
    output_bias,
    feed_gain,
    feed_shift,
    inner_weight,
    inner_bias,
    outer_weight,
    outer_bias,
):
    (
        gain_first,
        shift_first,
        query_full,
        bias_query,
        key_full,
        value_full,
        bias_value,
        output_full,
        bias_output,
        gain_second,
        shift_second,
        inner_full,
        bias_inner,
        outer_full,
        bias_outer,
    ) = (
        lax.all_gather(mix_gain, "dp", axis=0, tiled=True),
        lax.all_gather(mix_shift, "dp", axis=0, tiled=True),
        lax.all_gather(query_weight, "dp", axis=0, tiled=True),
        lax.all_gather(query_bias, "dp", axis=0, tiled=True),
        lax.all_gather(key_weight, "dp", axis=0, tiled=True),
        lax.all_gather(value_weight, "dp", axis=0, tiled=True),
        lax.all_gather(value_bias, "dp", axis=0, tiled=True),
        lax.all_gather(output_weight, "dp", axis=0, tiled=True),
        lax.all_gather(output_bias, "dp", axis=0, tiled=True),
        lax.all_gather(feed_gain, "dp", axis=0, tiled=True),
        lax.all_gather(feed_shift, "dp", axis=0, tiled=True),
        lax.all_gather(inner_weight, "dp", axis=0, tiled=True),
        lax.all_gather(inner_bias, "dp", axis=0, tiled=True),
        lax.all_gather(outer_weight, "dp", axis=0, tiled=True),
        lax.all_gather(outer_bias, "dp", axis=0, tiled=True),
    )
    clip_count = layer_input.shape[0]
    feature_count = layer_input.shape[2]
    normed_one, rstd_one, lowered_one = layer_norm(layer_input, gain_first, shift_first)
    gathered_one = lax.all_gather(lowered_one, "tensor", axis=1, tiled=True)
    frames = gathered_one.shape[1]
    flat_one = gathered_one.reshape(clip_count * frames, feature_count)
    vector_query = bias_query.astype(jnp.float32).T.reshape(-1)
    vector_value = bias_value.astype(jnp.float32).T.reshape(-1)
    vector_inner = bias_inner.astype(jnp.float32).T.reshape(-1)
    width = query_full.shape[1]
    queries = (matmul(flat_one, query_full) + vector_query).astype(jnp.bfloat16)
    key_rows = matmul(flat_one, key_full).astype(jnp.bfloat16)
    values = (matmul(flat_one, value_full) + vector_value).astype(jnp.bfloat16)
    clip_queries = queries.reshape(clip_count, frames, width)
    clip_keys = key_rows.reshape(clip_count, frames, width)
    clip_values = values.reshape(clip_count, frames, width)
    context, log_total = lax.map(attend, (clip_queries, clip_keys, clip_values))
    flat_context = context.reshape(clip_count * frames, width)
    attn_partial = matmul(flat_context, output_full.T).reshape(clip_count, frames, feature_count)
    attn_share = lax.psum_scatter(
        attn_partial.astype(jnp.bfloat16), "tensor", scatter_dimension=1, tiled=True
    ).astype(jnp.float32)
    mixed = layer_input + attn_share + bias_output.astype(jnp.float32)
    normed_two, rstd_two, lowered_two = layer_norm(mixed, gain_second, shift_second)
    gathered_two = lax.all_gather(lowered_two, "tensor", axis=1, tiled=True)
    flat_two = gathered_two.reshape(clip_count * frames, feature_count)
    preact = matmul(flat_two, inner_full) + vector_inner
    hidden = gelu_value(preact).astype(jnp.bfloat16)
    feed_partial = matmul(hidden, outer_full.T).reshape(clip_count, frames, feature_count)
    feed_share = lax.psum_scatter(
        feed_partial.astype(jnp.bfloat16), "tensor", scatter_dimension=1, tiled=True
    ).astype(jnp.float32)
    layer_output = mixed + feed_share + bias_outer.astype(jnp.float32)
    cot_low = out_cotangent.astype(jnp.bfloat16)
    cot_all = lax.all_gather(cot_low, "tensor", axis=1, tiled=True).reshape(
        clip_count * frames, feature_count
    )
    preact_grad = matmul(cot_all, outer_full) * gelu_slope(preact)
    preact_low = preact_grad.astype(jnp.bfloat16)
    outer_grad = token_product(cot_all, hidden)
    inner_grad = token_product(flat_two, preact_low)
    inner_bias_part = jnp.sum(preact_grad, axis=0).reshape(-1, HD).T
    norm_two_part = matmul(preact_low, inner_full.T).reshape(clip_count, frames, feature_count)
    norm_two_grad = lax.psum_scatter(
        norm_two_part.astype(jnp.bfloat16), "tensor", scatter_dimension=1, tiled=True
    ).astype(jnp.float32)
    feed_gain_part = jnp.sum(norm_two_grad * normed_two, axis=(0, 1))
    feed_shift_part = jnp.sum(norm_two_grad, axis=(0, 1))
    mixed_grad = out_cotangent + norm_backward(norm_two_grad, normed_two, rstd_two, gain_second)
    outer_bias_part = jnp.sum(out_cotangent, axis=(0, 1))
    output_bias_part = jnp.sum(mixed_grad, axis=(0, 1))
    mixed_low = mixed_grad.astype(jnp.bfloat16)
    mixed_all = lax.all_gather(mixed_low, "tensor", axis=1, tiled=True).reshape(
        clip_count * frames, feature_count
    )
    output_grad = token_product(mixed_all, flat_context)
    context_grad = (
        matmul(mixed_all, output_full).astype(jnp.bfloat16).reshape(clip_count, frames, width)
    )
    query_grad, key_low, value_grad = lax.map(
        attend_back, (clip_queries, clip_keys, clip_values, context_grad, log_total)
    )
    query_grad = query_grad.reshape(clip_count * frames, width)
    key_low = key_low.reshape(clip_count * frames, width)
    value_grad = value_grad.reshape(clip_count * frames, width)
    query_low = query_grad.astype(jnp.bfloat16)
    value_low = value_grad.astype(jnp.bfloat16)
    query_grad_part = token_product(flat_one, query_low)
    key_grad_part = token_product(flat_one, key_low)
    value_grad_part = token_product(flat_one, value_low)
    query_bias_part = jnp.sum(query_grad, axis=0).reshape(-1, HD).T
    value_bias_part = jnp.sum(value_grad, axis=0).reshape(-1, HD).T
    norm_one_part = (
        matmul(query_low, query_full.T)
        + matmul(key_low, key_full.T)
        + matmul(value_low, value_full.T)
    )
    norm_one_grad = lax.psum_scatter(
        norm_one_part.reshape(clip_count, frames, feature_count).astype(jnp.bfloat16),
        "tensor",
        scatter_dimension=1,
        tiled=True,
    ).astype(jnp.float32)
    mix_gain_part = jnp.sum(norm_one_grad * normed_one, axis=(0, 1))
    mix_shift_part = jnp.sum(norm_one_grad, axis=(0, 1))
    input_grad = mixed_grad + norm_backward(norm_one_grad, normed_one, rstd_one, gain_first)
    (
        query_weight_grad,
        query_bias_grad,
        key_weight_grad,
        value_weight_grad,
        value_bias_grad,
        output_weight_grad,
        inner_weight_grad,
        inner_bias_grad,
        outer_weight_grad,
    ) = (
        lax.psum_scatter(query_grad_part, "dp", scatter_dimension=0, tiled=True),
        lax.psum_scatter(query_bias_part, "dp", scatter_dimension=0, tiled=True),
        lax.psum_scatter(key_grad_part, "dp", scatter_dimension=0, tiled=True),
        lax.psum_scatter(value_grad_part, "dp", scatter_dimension=0, tiled=True),
        lax.psum_scatter(value_bias_part, "dp", scatter_dimension=0, tiled=True),
        lax.psum_scatter(output_grad, "dp", scatter_dimension=0, tiled=True),
        lax.psum_scatter(inner_grad, "dp", scatter_dimension=0, tiled=True),
        lax.psum_scatter(inner_bias_part, "dp", scatter_dimension=0, tiled=True),
        lax.psum_scatter(outer_grad, "dp", scatter_dimension=0, tiled=True),
    )
    (
        mix_gain_grad,
        mix_shift_grad,
        output_bias_grad,
        feed_gain_grad,
        feed_shift_grad,
        outer_bias_grad,
    ) = (
        lax.psum_scatter(mix_gain_part, ("dp", "tensor"), scatter_dimension=0, tiled=True),
        lax.psum_scatter(mix_shift_part, ("dp", "tensor"), scatter_dimension=0, tiled=True),
        lax.psum_scatter(output_bias_part, ("dp", "tensor"), scatter_dimension=0, tiled=True),
        lax.psum_scatter(feed_gain_part, ("dp", "tensor"), scatter_dimension=0, tiled=True),
        lax.psum_scatter(feed_shift_part, ("dp", "tensor"), scatter_dimension=0, tiled=True),
        lax.psum_scatter(outer_bias_part, ("dp", "tensor"), scatter_dimension=0, tiled=True),
    )
    return (
        layer_output,
        input_grad,
        mix_gain_grad,
        mix_shift_grad,
        query_weight_grad,
        query_bias_grad,
        key_weight_grad,
        value_weight_grad,
        value_bias_grad,
        output_weight_grad,
        output_bias_grad,
        feed_gain_grad,
        feed_shift_grad,
        inner_weight_grad,
        inner_bias_grad,
        outer_weight_grad,
        outer_bias_grad,
    )


def solution(mesh):
    placed = (
        P("dp", "tensor", None),
        P("dp", "tensor", None),
        P("dp"),
        P("dp"),
        P("dp", "tensor"),
        P("dp", "tensor"),
        P("dp", "tensor"),
        P("dp", "tensor"),
        P("dp", "tensor"),
        P("dp", "tensor"),
        P("dp"),
        P("dp"),
        P("dp"),
        P("dp", "tensor"),
        P("dp", "tensor"),
        P("dp", "tensor"),
        P("dp"),
    )
    return jax.shard_map(
        on_device,
        mesh=mesh,
        in_specs=placed,
        out_specs=(
            P("dp", "tensor", None),
            P("dp", "tensor", None),
            P(("dp", "tensor")),
            P(("dp", "tensor")),
            P("dp", "tensor"),
            P("dp", "tensor"),
            P("dp", "tensor"),
            P("dp", "tensor"),
            P("dp", "tensor"),
            P("dp", "tensor"),
            P(("dp", "tensor")),
            P(("dp", "tensor")),
            P(("dp", "tensor")),
            P("dp", "tensor"),
            P("dp", "tensor"),
            P("dp", "tensor"),
            P(("dp", "tensor")),
        ),
        check_vma=False,
    )
```

profile of v0, /device:TPU:0, one launch (start us, length us, event | category | flops | bytes accessed | tf_op | source)
XLA Modules:
  0.0 955.9 jit_solution(9160846206304437627)
XLA Ops:
  17.8 38.8 %all-reduce.17 = (bf16[768]{0:T(1024)(128)(2,1)S(1)}, bf16[768]{0:T(1024)(128)(2,1)S(1)}, bf16[768]{0:T(1024)(128)(2,1)S(1)}, bf16[768]{0:T(1024)(128)(2,1)S(1)}...) all-reduce(bf16[768]{0:T(1024)(128)(2,1)S(1)} %dynamic-update-slice., ...), channel_id=1, replica_groups=mesh['dp'=8,'tensor'=4] {'dp'}, use_global_device_ids=true, to_apply=%add.1 | all-reduce | flops 4608 | bytes 18432
  58.8 16.6 %all-gather.1 = bf16[8,8,3]{1,2,0:T(4,128)(2,1)S(1)} all-gather(bf16[1,8,3]{1,2,0:T(4,128)(2,1)S(1)} %bitcast.145), channel_id=1, replica_groups=mesh['dp'=8,'tensor'=4] {'dp'}, dimensions={0}, use_global_device_ids=true | all-gather | bytes 432 | tf_op jit(solution)/shard_map/all_gather | solution.py:146
  75.6 17.9 %all-gather = bf16[8,8,3]{1,2,0:T(4,128)(2,1)S(1)} all-gather(bf16[1,8,3]{1,2,0:T(4,128)(2,1)S(1)} %bitcast.146), channel_id=1, replica_groups=mesh['dp'=8,'tensor'=4] {'dp'}, dimensions={0}, use_global_device_ids=true | all-gather | bytes 432 | tf_op jit(solution)/shard_map/all_gather | solution.py:149
  93.7 31.1 %all_gather.62 = bf16[768,192]{1,0:T(8,128)(2,1)S(1)} all-gather(bf16[96,192]{1,0:T(8,128)(2,1)S(1)} %copy-done.22), channel_id=1, replica_groups=mesh['dp'=8,'tensor'=4] {'dp'}, dimensions={0}, use_global_device_ids=true | all-gather | bytes 331776 | tf_op jit(solution)/shard_map/all_gather | solution.py:145
  124.8 31.1 %all_gather.64 = bf16[768,192]{1,0:T(8,128)(2,1)S(1)} all-gather(bf16[96,192]{1,0:T(8,128)(2,1)S(1)} %copy-done.23), channel_id=1, replica_groups=mesh['dp'=8,'tensor'=4] {'dp'}, dimensions={0}, use_global_device_ids=true | all-gather | bytes 331776 | tf_op jit(solution)/shard_map/all_gather | solution.py:147
  155.9 31.1 %all_gather.60 = bf16[768,192]{1,0:T(8,128)(2,1)S(1)} all-gather(bf16[96,192]{1,0:T(8,128)(2,1)S(1)} %copy-done.24), channel_id=1, replica_groups=mesh['dp'=8,'tensor'=4] {'dp'}, dimensions={0}, use_global_device_ids=true | all-gather | bytes 331776 | tf_op jit(solution)/shard_map/all_gather | solution.py:148
  187.0 31.0 %all_gather.65 = bf16[768,192]{1,0:T(8,128)(2,1)S(1)} all-gather(bf16[96,192]{1,0:T(8,128)(2,1)S(1)} %copy-done.25), channel_id=1, replica_groups=mesh['dp'=8,'tensor'=4] {'dp'}, dimensions={0}, use_global_device_ids=true | all-gather | bytes 331776 | tf_op jit(solution)/shard_map/all_gather | solution.py:150
  236.3 23.1 %reduce-scatter.16.cloned.1.call-done = bf16[1,256,768]{2,1,0:T(8,128)(2,1)} async-done(((bf16[1,1024,768]{2,1,0:T(8,128)(2,1)}), bf16[1,256,768]{2,1,0:T(8,128)(2,1)}) %reduce-scatter.16.cloned.1.call-update) | async-done | bytes 393232 | tf_op jit(solution)/shard_map/reduce_scatter | solution.py:178
  267.0 26.2 %all_gather.71 = bf16[64,12]{1,0:T(8,128)(2,1)S(1)} all-gather(bf16[8,12]{1,0:T(8,128)(2,1)} %param.31), channel_id=1, replica_groups=mesh['dp'=8,'tensor'=4] {'dp'}, dimensions={0}, use_global_device_ids=true | all-gather | bytes 1728 | tf_op jit(solution)/shard_map/all_gather | solution.py:155
  302.1 37.3 %all-gather.15.cloned.1.call-done = bf16[768,768]{1,0:T(8,128)(2,1)} async-done(((bf16[96,768]{1,0:T(8,128)(2,1)}), bf16[768,768]{1,0:T(8,128)(2,1)}) %all-gather.15.cloned.1.call-update) | async-done | bytes 1179664 | tf_op jit(solution)/shard_map/all_gather | solution.py:156
  339.4 20.3 %all-gather.17.cloned.1.call-done = bf16[1,1024,768]{2,1,0:T(8,128)(2,1)} async-done(((bf16[1,256,768]{2,1,0:T(8,128)(2,1)}), bf16[1,1024,768]{2,1,0:T(8,128)(2,1)}) %all-gather.17.cloned.1.call-update) | async-done | bytes 1572880 | tf_op jit(solution)/shard_map/all_gather | solution.py:193
  374.7 22.6 %reduce-scatter.20.cloned.1.call-done = bf16[1,256,768]{2,1,0:T(8,128)(2,1)} async-done(((bf16[1,1024,768]{2,1,0:T(8,128)(2,1)}), bf16[1,256,768]{2,1,0:T(8,128)(2,1)}) %reduce-scatter.20.cloned.1.call-update) | async-done | bytes 393232 | tf_op jit(solution)/shard_map/reduce_scatter | solution.py:202
  399.9 28.0 %reduce-scatter.18.cloned.1.call-done = bf16[1,256,768]{2,1,0:T(8,128)(2,1)} async-done(((bf16[1,1024,768]{2,1,0:T(8,128)(2,1)}), bf16[1,256,768]{2,1,0:T(8,128)(2,1)}) %reduce-scatter.18.cloned.1.call-update) | async-done | bytes 393232 | tf_op jit(solution)/shard_map/reduce_scatter | solution.py:188
  433.0 19.6 %all-gather.19.cloned.1.call-done = bf16[1,1024,768]{2,1,0:T(8,128)(2,1)} async-done(((bf16[1,256,768]{2,1,0:T(8,128)(2,1)}), bf16[1,1024,768]{2,1,0:T(8,128)(2,1)}) %all-gather.19.cloned.1.call-update) | async-done | bytes 1572880 | tf_op jit(solution)/shard_map/all_gather | solution.py:211
  454.6 7.5 fusion.104
  468.5 19.8 %fusion.70 = bf16[3,64,1024]{2,1,0:T(8,128)(2,1)} fusion(bf16[1024,3,64]{0,2,1:T(8,128)(2,1)S(1)} %bitcast.135, f32[3,1024,1024]{1,2,0:T(8,128)} %fusion.111, f32[3,1024,1024]{1,2,0:T(8,128)} %copy-done, f32[3,1024]{1,0:T(4,128)S(1)} %log_add_fusion), kind=kOutput, calls=%fused_computation.61 | convolution fusion | flops 431165440 | bytes 25964544 | tf_op jit(solution)/shard_map/while/body/eval_jaxpr/hqk,qhd->khd/dot_general | solution.py:97
  488.3 20.0 %fusion.105 = (f32[3,64]{1,0:T(4,128)}, bf16[1024,3,64]{0,2,1:T(8,128)(2,1)}) fusion(bf16[1024,3,64]{0,2,1:T(8,128)(2,1)S(1)} %bitcast.133, f32[3,1024,1024]{1,2,0:T(8,128)} %fusion.111, f32[3,1024,1024]{1,2,0:T(8,128)} %copy-done, f32[3,1024]{1,0:T(4,128)S(1)} %log_add_fusion), kind=kOutput, calls=%fused_computation.118 | convolution fusion | flops 431361856 | bytes 25965312 | tf_op jit(solution)/shard_map/while/body/eval_jaxpr/hqk,khd->qhd/dot_general | solution.py:94
  535.0 37.5 %all-reduce.16 = (f32[64,3]{0,1:T(4,128)S(1)}, f32[64,3]{0,1:T(4,128)S(1)}, f32[64,12]{0,1:T(8,128)S(1)}) all-reduce(f32[64,3]{0,1:T(4,128)} %bitcast.144, f32[64,3]{0,1:T(4,128)} %bitcast.143, f32[64,12]{0,1:T(8,128)S(1)} %bitcast.140), channel_id=9, replica_groups=mesh['dp'=8,'tensor'=4] {'dp'}, use_global_device_ids=true, to_apply=%region_21.22.clone | all-reduce | flops 1152 | bytes 9216
  576.0 37.7 %all-reduce.15 = (f32[768]{0:T(1024)S(1)}, f32[768]{0:T(1024)S(1)}, f32[768]{0:T(1024)S(1)}, f32[768]{0:T(1024)S(1)}, f32[768]{0:T(1024)S(1)}, /*index=5*/f32[768]{0:T(1024)S(1)}) all-reduce(f32[768]{0:T(1024)S(1)} %get-tuple-element.132, f32[768]{0:T(1024)S(1)} %get-tuple-element.137, ...), channel_id=6, replica_groups=mesh['dp'=8,'tensor'=4] {'dp','tensor'}, use_global_device_ids=true, to_apply=%region_16.17.clone | all-reduce | flops 4608 | bytes 36864
  619.4 66.7 %reduce-scatter.34.cloned.1.call-done = f32[96,768]{1,0:T(8,128)} async-done(((f32[768,768]{1,0:T(8,128)}), f32[96,768]{1,0:T(8,128)}) %reduce-scatter.34.cloned.1.call-update) | async-done | bytes 294928
  686.1 65.4 %reduce-scatter.30.cloned.1.call-done = f32[96,192]{1,0:T(8,128)} async-done(((f32[768,192]{1,0:T(8,128)}), f32[96,192]{1,0:T(8,128)}) %reduce-scatter.30.cloned.1.call-update) | async-done | bytes 73744 | tf_op jit(solution)/shard_map/reduce_scatter | solution.py:261
  751.5 65.8 %reduce-scatter.28.cloned.1.call-done = f32[96,192]{1,0:T(8,128)} async-done(((f32[768,192]{1,0:T(8,128)}), f32[96,192]{1,0:T(8,128)}) %reduce-scatter.28.cloned.1.call-update) | async-done | bytes 73744 | tf_op jit(solution)/shard_map/reduce_scatter | solution.py:259
  817.3 65.4 %reduce-scatter.26.cloned.1.call-done = f32[96,192]{1,0:T(8,128)} async-done(((f32[768,192]{1,0:T(8,128)}), f32[96,192]{1,0:T(8,128)}) %reduce-scatter.26.cloned.1.call-update) | async-done | bytes 73744 | tf_op jit(solution)/shard_map/reduce_scatter | solution.py:258
  882.7 65.8 %reduce-scatter.24.cloned.1.call-done = f32[96,192]{1,0:T(8,128)} async-done(((f32[768,192]{1,0:T(8,128)}), f32[96,192]{1,0:T(8,128)}) %reduce-scatter.24.cloned.1.call-update) | async-done | bytes 73744 | tf_op jit(solution)/shard_map/reduce_scatter | solution.py:256
  (189 shorter events, 112.2 us)
Async XLA Ops:
  8.0 85.7 %copy-start.22 = (bf16[96,192]{1,0:T(8,128)(2,1)S(1)}, bf16[96,192]{1,0:T(8,128)(2,1)}, u32[]{:S(2)}) copy-start(bf16[96,192]{1,0:T(8,128)(2,1)} %param.21) | copy-start | bytes 110596
  8.1 116.8 %copy-start.23 = (bf16[96,192]{1,0:T(8,128)(2,1)S(1)}, bf16[96,192]{1,0:T(8,128)(2,1)}, u32[]{:S(2)}) copy-start(bf16[96,192]{1,0:T(8,128)(2,1)} %param.23) | copy-start | bytes 110596
  8.1 147.8 %copy-start.24 = (bf16[96,192]{1,0:T(8,128)(2,1)S(1)}, bf16[96,192]{1,0:T(8,128)(2,1)}, u32[]{:S(2)}) copy-start(bf16[96,192]{1,0:T(8,128)(2,1)} %param.24) | copy-start | bytes 110596
  8.1 178.9 %copy-start.25 = (bf16[96,192]{1,0:T(8,128)(2,1)S(1)}, bf16[96,192]{1,0:T(8,128)(2,1)}, u32[]{:S(2)}) copy-start(bf16[96,192]{1,0:T(8,128)(2,1)} %param.26) | copy-start | bytes 110596
  8.1 209.9 %all-gather.9.cloned.1.call-start = ((), (), s32[]{:S(2)}) async-start(), calls=%async_computation.10 | async-start | bytes 1966080 | tf_op jit(solution)/shard_map/all_gather | solution.py:162
  56.6 68.2 %copy-start.20 = (f32[768]{0:T(1024)}, f32[768]{0:T(1024)S(1)}, u32[]{:S(2)}) copy-start(f32[768]{0:T(1024)S(1)} %convert_element_type.132) | copy-start | bytes 9220
  58.8 200.6 %reduce-scatter.16.cloned.1.call-start = ((), (), s32[]{:S(2)}) async-start(), calls=%async_computation.11 | async-start | bytes 1966080 | tf_op jit(solution)/shard_map/reduce_scatter | solution.py:178
  124.8 99.5 %copy-start.12 = (bf16[768,192]{1,0:T(8,128)(2,1)}, bf16[768,192]{1,0:T(8,128)(2,1)S(1)}, u32[]{:S(2)}) copy-start(bf16[768,192]{1,0:T(8,128)(2,1)S(1)} %all_gather.62) | copy-start | bytes 884740
  155.9 68.4 %copy-start.10 = (bf16[768,192]{1,0:T(8,128)(2,1)}, bf16[768,192]{1,0:T(8,128)(2,1)S(1)}, u32[]{:S(2)}) copy-start(bf16[768,192]{1,0:T(8,128)(2,1)S(1)} %all_gather.64) | copy-start | bytes 884740
  233.9 62.7 %all-gather.13.cloned.1.call-start = ((), (), s32[]{:S(2)}) async-start(), calls=%async_computation.13 | async-start | bytes 1327104 | tf_op jit(solution)/shard_map/all_gather | solution.py:154
  234.5 62.1 %all-gather.11.cloned.1.call-start = ((), (), s32[]{:S(2)}) async-start(), calls=%async_computation.12 | async-start | bytes 1966080 | tf_op jit(solution)/shard_map/all_gather | solution.py:183
  263.4 76.0 %all-gather.15.cloned.1.call-start = ((), (), s32[]{:S(2)}) async-start(), calls=%async_computation.14 | async-start | bytes 1327104 | tf_op jit(solution)/shard_map/all_gather | solution.py:156
  264.0 95.7 %all-gather.17.cloned.1.call-start = ((), (), s32[]{:S(2)}) async-start(), calls=%async_computation.16 | async-start | bytes 1966080 | tf_op jit(solution)/shard_map/all_gather | solution.py:193
  266.9 130.4 %reduce-scatter.20.cloned.1.call-start = ((), (), s32[]{:S(2)}) async-start(), calls=%async_computation.17 | async-start | bytes 1966080 | tf_op jit(solution)/shard_map/reduce_scatter | solution.py:202
  369.0 59.0 %reduce-scatter.18.cloned.1.call-start = ((), (), s32[]{:S(2)}) async-start(), calls=%async_computation.15 | async-start | bytes 1966080 | tf_op jit(solution)/shard_map/reduce_scatter | solution.py:188
  373.4 79.1 %all-gather.19.cloned.1.call-start = ((), (), s32[]{:S(2)}) async-start(), calls=%async_computation.18 | async-start | bytes 1966080 | tf_op jit(solution)/shard_map/all_gather | solution.py:211
  432.9 141.7 %reduce-scatter.22.cloned.1.call-start = ((), (), s32[]{:S(2)}) async-start(), calls=%async_computation.19 | async-start | bytes 1966080 | tf_op jit(solution)/shard_map/reduce_scatter | solution.py:236
  512.6 106.8 %reduce-scatter.32.cloned.1.call-start = ((), (), s32[]{:S(2)}) async-start(), calls=%async_computation.24 | async-start | bytes 2654208 | tf_op jit(solution)/shard_map/reduce_scatter | solution.py:262
  517.4 168.7 %reduce-scatter.34.cloned.1.call-start = ((), (), s32[]{:S(2)}) async-start(), calls=%async_computation.25 | async-start | bytes 2654208
  525.4 226.1 %reduce-scatter.30.cloned.1.call-start = ((), (), s32[]{:S(2)}) async-start(), calls=%async_computation.23 | async-start | bytes 884736 | tf_op jit(solution)/shard_map/reduce_scatter | solution.py:261
  528.6 288.7 %reduce-scatter.28.cloned.1.call-start = ((), (), s32[]{:S(2)}) async-start(), calls=%async_computation.22 | async-start | bytes 884736 | tf_op jit(solution)/shard_map/reduce_scatter | solution.py:259
  530.3 352.4 %reduce-scatter.26.cloned.1.call-start = ((), (), s32[]{:S(2)}) async-start(), calls=%async_computation.21 | async-start | bytes 884736 | tf_op jit(solution)/shard_map/reduce_scatter | solution.py:258
  531.9 85.3 %copy-start.4 = (f32[1,256,768]{2,1,0:T(8,128)S(1)}, f32[1,256,768]{2,1,0:T(8,128)}, u32[]{:S(2)}) copy-start(f32[1,256,768]{2,1,0:T(8,128)} %copy-done.3) | copy-start | bytes 2359300
  531.9 416.6 %reduce-scatter.24.cloned.1.call-start = ((), (), s32[]{:S(2)}) async-start(), calls=%async_computation.20 | async-start | bytes 884736 | tf_op jit(solution)/shard_map/reduce_scatter | solution.py:256
  (27 other events, 466.4 us)
Sparse Core Ops, SparseCore 0:
  58.9 16.9 all-gather.8
  234.0 25.3 reduce-scatter.15
  369.1 28.1 reduce-scatter.19
  399.7 28.1 reduce-scatter.17
Sparse Core Ops, SparseCore 1:
  236.8 38.6 all-gather.12
  277.6 18.0 all-gather.10
  297.9 41.5 all-gather.14
  341.7 18.0 all-gather.16
  433.0 19.5 all-gather.18
  512.7 28.1 reduce-scatter.21
  544.7 69.3 reduce-scatter.31
  618.0 68.0 reduce-scatter.33
  689.9 61.6 reduce-scatter.29
  755.8 61.5 reduce-scatter.27
  821.1 61.5 reduce-scatter.25
  886.9 61.5 reduce-scatter.23
where the time goes:
time: 965 us; the launch traced here: 956 us
  waiting for transfers between devices  481 us (50%)
  blocking collectives  299 us (31%)
  matrix products  106 us (11%)
  other arithmetic  26.7 us (3%)
  local copies, waits for them, and re-layouts  24.5 us (3%)
  between operations  17.4 us (2%)
    unnamed x3, blocking collectives  114 us
    unnamed x17, waiting for transfers between devices  67.5 us
    reduce_scatter x1, waiting for transfers between devices, on_device(): lax.psum_scatter(query_grad_part, 'dp', scatter_dimension=0, tiled=True)  65.8 us
    reduce_scatter x1, waiting for transfers between devices, on_device(): lax.psum_scatter(value_grad_part, 'dp', scatter_dimension=0, tiled=True)  65.8 us
    reduce_scatter x1, waiting for transfers between devices, on_device(): lax.psum_scatter(output_grad, 'dp', scatter_dimension=0, tiled=True)  65.4 us
    reduce_scatter x1, waiting for transfers between devices, on_device(): lax.psum_scatter(key_grad_part, 'dp', scatter_dimension=0, tiled=True)  65.4 us
    all_gather x1, waiting for transfers between devices, on_device(): lax.all_gather(outer_weight, 'dp', axis=0, tiled=True)  37.3 us
    dot_general x12, matrix products, matmul(): return jnp.dot(left, right, preferred_element_type=jnp.float32)  31.2 us
  transfers between devices with their start and end apart: 16, of which 11 were waited for; matrix products, arithmetic and copies ran while one was open for 6% of the time, Pallas kernels for 0%

commit v1 on v0

--- a/solution.py
+++ b/solution.py
@@ -8,6 +8,28 @@
 EPS = 1e-05
 ROOT_HALF = 0.7071067811865476
 DENSITY_NORM = 0.3989422804014327
+
+
+def laid_out(blocks, dim):
+    blocks = jnp.moveaxis(blocks, 0, dim)
+    lengths = blocks.shape
+    return blocks.reshape(*lengths[:dim], lengths[dim] * lengths[dim + 1], *lengths[dim + 2 :])
+
+
+def collect(x, axis, dim):
+    peers = lax.axis_size(axis)
+    pairs = [(i, (i + 1) % peers) for i in range(peers)]
+    back = [(b, a) for a, b in pairs]
+    lower, upper = ([], [])
+    for step in range(peers - 1):
+        if step % 2 == 0:
+            lower.append(lax.ppermute(lower[-1] if lower else x, axis, pairs))
+        else:
+            upper.append(lax.ppermute(upper[-1] if upper else x, axis, back))
+    parts = jnp.stack([*lower[::-1], x, *upper])
+    shift = lax.axis_index(axis) - len(lower)
+    parts = parts[(jnp.arange(peers) - shift) % peers]
+    return laid_out(parts, dim)
 
 
 def layer_norm(block, gain, shift):
@@ -147,7 +169,7 @@
         lax.all_gather(key_weight, "dp", axis=0, tiled=True),
         lax.all_gather(value_weight, "dp", axis=0, tiled=True),
         lax.all_gather(value_bias, "dp", axis=0, tiled=True),
-        lax.all_gather(output_weight, "dp", axis=0, tiled=True),
+        collect(output_weight, "dp", 0),
         lax.all_gather(output_bias, "dp", axis=0, tiled=True),
         lax.all_gather(feed_gain, "dp", axis=0, tiled=True),
         lax.all_gather(feed_shift, "dp", axis=0, tiled=True),

time: 965 us -> 950 us (0.984)
  blocking collectives: 299 us -> 265 us
  starting transfers between devices: 1.36 us -> 16.8 us
    all_gather x1 -> x0, blocking collectives: 31 us -> none  [on_device(): lax.all_gather(output_weight, 'dp', axis=0, tiled=True)]
    ppermute x0 -> x7, starting transfers between devices: none -> 15.9 us  [the longest x3 10.9 us: collect(): upper.append(lax.ppermute(upper[-1] if upper else x, axis, back))]
    unnamed x94 -> x101, local copies, waits for them, and re-layouts: 20.7 us -> 20.7 us
  transfers between devices with their start and end apart: 16 -> 23, of which waited for: 11 -> 14; matrix products, arithmetic and copies ran while one was open for 6% -> 7% of each run, Pallas kernels for 0% -> 0%
where the time goes in v1:
time: 950 us; the launch traced here: 945 us
  waiting for transfers between devices  488 us (51%)
  blocking collectives  265 us (28%)
  matrix products  106 us (11%)
  other arithmetic  26.7 us (3%)
  local copies, waits for them, and re-layouts  25.1 us (3%)
  between operations  17.5 us (2%)
  starting transfers between devices  16.8 us (2%)
    unnamed x3, blocking collectives  110 us
    unnamed x17, waiting for transfers between devices  67.4 us
    reduce_scatter x1, waiting for transfers between devices, on_device(): lax.psum_scatter(value_grad_part, 'dp', scatter_dimension=0, tiled=True)  65.8 us
    reduce_scatter x1, waiting for transfers between devices, on_device(): lax.psum_scatter(query_grad_part, 'dp', scatter_dimension=0, tiled=True)  65.8 us
    reduce_scatter x1, waiting for transfers between devices, on_device(): lax.psum_scatter(output_grad, 'dp', scatter_dimension=0, tiled=True)  65.4 us
    reduce_scatter x1, waiting for transfers between devices, on_device(): lax.psum_scatter(key_grad_part, 'dp', scatter_dimension=0, tiled=True)  65.4 us
    all_gather x1, waiting for transfers between devices, on_device(): lax.all_gather(outer_weight, 'dp', axis=0, tiled=True)  36.6 us
    dot_general x12, matrix products, matmul(): return jnp.dot(left, right, preferred_element_type=jnp.float32)  31.3 us
  transfers between devices with their start and end apart: 23, of which 14 were waited for; matrix products, arithmetic and copies ran while one was open for 7% of the time, Pallas kernels for 0%

profile of v1, /device:TPU:0, one launch (start us, length us, event | category | flops | bytes accessed | tf_op | source)
XLA Modules:
  0.0 945.4 jit_solution(1673623032962022)
XLA Ops:
  23.9 34.8 %all-reduce.17 = (bf16[768]{0:T(1024)(128)(2,1)S(1)}, bf16[768]{0:T(1024)(128)(2,1)S(1)}, bf16[768]{0:T(1024)(128)(2,1)S(1)}, bf16[768]{0:T(1024)(128)(2,1)S(1)}...) all-reduce(bf16[768]{0:T(1024)(128)(2,1)S(1)} %dynamic-update-slice., ...), channel_id=1, replica_groups=mesh['dp'=8,'tensor'=4] {'dp'}, use_global_device_ids=true, to_apply=%add.1 | all-reduce | flops 4608 | bytes 18432
  60.9 16.6 %all-gather.1 = bf16[8,8,3]{1,2,0:T(4,128)(2,1)S(1)} all-gather(bf16[1,8,3]{1,2,0:T(4,128)(2,1)S(1)} %bitcast.166), channel_id=1, replica_groups=mesh['dp'=8,'tensor'=4] {'dp'}, dimensions={0}, use_global_device_ids=true | all-gather | bytes 432 | tf_op jit(solution)/shard_map/all_gather | solution.py:168
  77.5 17.9 %all-gather = bf16[8,8,3]{1,2,0:T(4,128)(2,1)S(1)} all-gather(bf16[1,8,3]{1,2,0:T(4,128)(2,1)S(1)} %bitcast.167), channel_id=1, replica_groups=mesh['dp'=8,'tensor'=4] {'dp'}, dimensions={0}, use_global_device_ids=true | all-gather | bytes 432 | tf_op jit(solution)/shard_map/all_gather | solution.py:171
  95.4 31.1 %all_gather.59 = bf16[768,192]{1,0:T(8,128)(2,1)S(1)} all-gather(bf16[96,192]{1,0:T(8,128)(2,1)S(1)} %copy-done.22), channel_id=1, replica_groups=mesh['dp'=8,'tensor'=4] {'dp'}, dimensions={0}, use_global_device_ids=true | all-gather | bytes 331776 | tf_op jit(solution)/shard_map/all_gather | solution.py:167
  126.5 31.1 %all_gather.61 = bf16[768,192]{1,0:T(8,128)(2,1)S(1)} all-gather(bf16[96,192]{1,0:T(8,128)(2,1)S(1)} %copy-done.23), channel_id=1, replica_groups=mesh['dp'=8,'tensor'=4] {'dp'}, dimensions={0}, use_global_device_ids=true | all-gather | bytes 331776 | tf_op jit(solution)/shard_map/all_gather | solution.py:169
  157.7 31.0 %all_gather.57 = bf16[768,192]{1,0:T(8,128)(2,1)S(1)} all-gather(bf16[96,192]{1,0:T(8,128)(2,1)S(1)} %copy-done.24), channel_id=1, replica_groups=mesh['dp'=8,'tensor'=4] {'dp'}, dimensions={0}, use_global_device_ids=true | all-gather | bytes 331776 | tf_op jit(solution)/shard_map/all_gather | solution.py:170
  221.6 28.0 %reduce-scatter.16.cloned.1.call-done = bf16[1,256,768]{2,1,0:T(8,128)(2,1)} async-done(((bf16[1,1024,768]{2,1,0:T(8,128)(2,1)}), bf16[1,256,768]{2,1,0:T(8,128)(2,1)}) %reduce-scatter.16.cloned.1.call-update) | async-done | bytes 393232 | tf_op jit(solution)/shard_map/reduce_scatter | solution.py:200
  257.1 26.7 %all_gather.67 = bf16[64,12]{1,0:T(8,128)(2,1)S(1)} all-gather(bf16[8,12]{1,0:T(8,128)(2,1)} %param.31), channel_id=1, replica_groups=mesh['dp'=8,'tensor'=4] {'dp'}, dimensions={0}, use_global_device_ids=true | all-gather | bytes 1728 | tf_op jit(solution)/shard_map/all_gather | solution.py:177
  292.8 36.6 %all-gather.15.cloned.1.call-done = bf16[768,768]{1,0:T(8,128)(2,1)} async-done(((bf16[96,768]{1,0:T(8,128)(2,1)}), bf16[768,768]{1,0:T(8,128)(2,1)}) %all-gather.15.cloned.1.call-update) | async-done | bytes 1179664 | tf_op jit(solution)/shard_map/all_gather | solution.py:178
  329.4 20.3 %all-gather.17.cloned.1.call-done = bf16[1,1024,768]{2,1,0:T(8,128)(2,1)} async-done(((bf16[1,256,768]{2,1,0:T(8,128)(2,1)}), bf16[1,1024,768]{2,1,0:T(8,128)(2,1)}) %all-gather.17.cloned.1.call-update) | async-done | bytes 1572880 | tf_op jit(solution)/shard_map/all_gather | solution.py:215
  364.6 22.6 %reduce-scatter.20.cloned.1.call-done = bf16[1,256,768]{2,1,0:T(8,128)(2,1)} async-done(((bf16[1,1024,768]{2,1,0:T(8,128)(2,1)}), bf16[1,256,768]{2,1,0:T(8,128)(2,1)}) %reduce-scatter.20.cloned.1.call-update) | async-done | bytes 393232 | tf_op jit(solution)/shard_map/reduce_scatter | solution.py:224
  389.8 28.0 %reduce-scatter.18.cloned.1.call-done = bf16[1,256,768]{2,1,0:T(8,128)(2,1)} async-done(((bf16[1,1024,768]{2,1,0:T(8,128)(2,1)}), bf16[1,256,768]{2,1,0:T(8,128)(2,1)}) %reduce-scatter.18.cloned.1.call-update) | async-done | bytes 393232 | tf_op jit(solution)/shard_map/reduce_scatter | solution.py:210
  422.8 19.6 %all-gather.19.cloned.1.call-done = bf16[1,1024,768]{2,1,0:T(8,128)(2,1)} async-done(((bf16[1,256,768]{2,1,0:T(8,128)(2,1)}), bf16[1,1024,768]{2,1,0:T(8,128)(2,1)}) %all-gather.19.cloned.1.call-update) | async-done | bytes 1572880 | tf_op jit(solution)/shard_map/all_gather | solution.py:233
  444.5 7.5 fusion.106
  452.1 6.3 fusion.113
  458.4 19.7 %fusion.70 = bf16[3,64,1024]{2,1,0:T(8,128)(2,1)} fusion(bf16[1024,3,64]{0,2,1:T(8,128)(2,1)S(1)} %bitcast.156, f32[3,1024,1024]{1,2,0:T(8,128)} %fusion.113, f32[3,1024,1024]{1,2,0:T(8,128)} %copy-done, f32[3,1024]{1,0:T(4,128)S(1)} %log_add_fusion), kind=kOutput, calls=%fused_computation.62 | convolution fusion | flops 431165440 | bytes 25964544 | tf_op jit(solution)/shard_map/while/body/eval_jaxpr/hqk,qhd->khd/dot_general | solution.py:119
  478.1 20.0 %fusion.107 = (f32[3,64]{1,0:T(4,128)}, bf16[1024,3,64]{0,2,1:T(8,128)(2,1)}) fusion(bf16[1024,3,64]{0,2,1:T(8,128)(2,1)S(1)} %bitcast.154, f32[3,1024,1024]{1,2,0:T(8,128)} %fusion.113, f32[3,1024,1024]{1,2,0:T(8,128)} %copy-done, f32[3,1024]{1,0:T(4,128)S(1)} %log_add_fusion), kind=kOutput, calls=%fused_computation.134 | convolution fusion | flops 431361856 | bytes 25965312 | tf_op jit(solution)/shard_map/while/body/eval_jaxpr/hqk,khd->qhd/dot_general | solution.py:116
  524.8 37.5 %all-reduce.16 = (f32[64,3]{0,1:T(4,128)S(1)}, f32[64,3]{0,1:T(4,128)S(1)}, f32[64,12]{0,1:T(8,128)S(1)}) all-reduce(f32[64,3]{0,1:T(4,128)} %bitcast.165, f32[64,3]{0,1:T(4,128)} %bitcast.164, f32[64,12]{0,1:T(8,128)S(1)} %bitcast.161), channel_id=9, replica_groups=mesh['dp'=8,'tensor'=4] {'dp'}, use_global_device_ids=true, to_apply=%region_21.22.clone | all-reduce | flops 1152 | bytes 9216
  565.8 37.9 %all-reduce.15 = (f32[768]{0:T(1024)S(1)}, f32[768]{0:T(1024)S(1)}, f32[768]{0:T(1024)S(1)}, f32[768]{0:T(1024)S(1)}, f32[768]{0:T(1024)S(1)}, /*index=5*/f32[768]{0:T(1024)S(1)}) all-reduce(f32[768]{0:T(1024)S(1)} %get-tuple-element.132, f32[768]{0:T(1024)S(1)} %get-tuple-element.137, ...), channel_id=6, replica_groups=mesh['dp'=8,'tensor'=4] {'dp','tensor'}, use_global_device_ids=true, to_apply=%region_16.17.clone | all-reduce | flops 4608 | bytes 36864
  609.4 66.2 %reduce-scatter.34.cloned.1.call-done = f32[96,768]{1,0:T(8,128)} async-done(((f32[768,768]{1,0:T(8,128)}), f32[96,768]{1,0:T(8,128)}) %reduce-scatter.34.cloned.1.call-update) | async-done | bytes 294928
  675.6 65.4 %reduce-scatter.30.cloned.1.call-done = f32[96,192]{1,0:T(8,128)} async-done(((f32[768,192]{1,0:T(8,128)}), f32[96,192]{1,0:T(8,128)}) %reduce-scatter.30.cloned.1.call-update) | async-done | bytes 73744 | tf_op jit(solution)/shard_map/reduce_scatter | solution.py:283
  741.0 65.8 %reduce-scatter.28.cloned.1.call-done = f32[96,192]{1,0:T(8,128)} async-done(((f32[768,192]{1,0:T(8,128)}), f32[96,192]{1,0:T(8,128)}) %reduce-scatter.28.cloned.1.call-update) | async-done | bytes 73744 | tf_op jit(solution)/shard_map/reduce_scatter | solution.py:281
  806.9 65.4 %reduce-scatter.26.cloned.1.call-done = f32[96,192]{1,0:T(8,128)} async-done(((f32[768,192]{1,0:T(8,128)}), f32[96,192]{1,0:T(8,128)}) %reduce-scatter.26.cloned.1.call-update) | async-done | bytes 73744 | tf_op jit(solution)/shard_map/reduce_scatter | solution.py:280
  872.2 65.8 %reduce-scatter.24.cloned.1.call-done = f32[96,192]{1,0:T(8,128)} async-done(((f32[768,192]{1,0:T(8,128)}), f32[96,192]{1,0:T(8,128)}) %reduce-scatter.24.cloned.1.call-update) | async-done | bytes 73744 | tf_op jit(solution)/shard_map/reduce_scatter | solution.py:278
  (213 shorter events, 126.1 us)
Async XLA Ops:
  8.0 194.3 %copy-start.25 = (bf16[96,192]{1,0:T(8,128)(2,1)S(1)}, bf16[96,192]{1,0:T(8,128)(2,1)}, u32[]{:S(2)}) copy-start(bf16[96,192]{1,0:T(8,128)(2,1)} %param.26) | copy-start | bytes 110596
  8.1 195.1 %all-gather.9.cloned.1.call-start = ((), (), s32[]{:S(2)}) async-start(), calls=%async_computation.10 | async-start | bytes 1966080 | tf_op jit(solution)/shard_map/all_gather | solution.py:184
  8.1 149.5 %collective-permute-start = (bf16[96,192]{1,0:T(8,128)(2,1)}, bf16[96,192]{1,0:T(8,128)(2,1)S(1)}, u32[]{:S(2)}, u32[]{:S(2)}) collective-permute-start(bf16[96,192]{1,0:T(8,128)(2,1)} %param.26), channel_id=1, source_target_pairs={{0,4},{4,8},{8,12},{12,16},{16,20},{20,24},{24,28},{28,0},{1,5},{5... | collective-permute-start | bytes 110600 | tf_op jit(solution)/shard_map/ppermute | solution.py:26
  11.1 179.6 %collective-permute-start.4 = (bf16[96,192]{1,0:T(8,128)(2,1)}, bf16[96,192]{1,0:T(8,128)(2,1)S(1)}, u32[]{:S(2)}, u32[]{:S(2)}) collective-permute-start(bf16[96,192]{1,0:T(8,128)(2,1)} %param.26), channel_id=1, source_target_pairs={{4,0},{8,4},{12,8},{16,12},{20,16},{24,20},{28,24},{0,28},{5,1},{9... | collective-permute-start | bytes 110600 | tf_op jit(solution)/shard_map/ppermute | solution.py:28
  60.8 188.7 %reduce-scatter.16.cloned.1.call-start = ((), (), s32[]{:S(2)}) async-start(), calls=%async_computation.11 | async-start | bytes 1966080 | tf_op jit(solution)/shard_map/reduce_scatter | solution.py:200
  157.6 31.1 %collective-permute-start.1 = (bf16[96,192]{1,0:T(8,128)(2,1)S(1)}, bf16[96,192]{1,0:T(8,128)(2,1)S(1)}, u32[]{:S(2)}, u32[]{:S(2)}) collective-permute-start(bf16[96,192]{1,0:T(8,128)(2,1)S(1)} %collective-permute-done), channel_id=1, source_target_pairs={{0,4},{4,8},{8,12},{12,16},{16,20},{20,24},{24,28},{28,0},{1,5},{5... | collective-permute-start | bytes 110600 | tf_op jit(solution)/shard_map/ppermute | solution.py:26
  188.7 6.8 collective-permute-start.2
  190.7 5.2 collective-permute-start.5
  195.5 6.8 collective-permute-start.3
  195.9 6.7 collective-permute-start.6
  219.2 68.1 %all-gather.13.cloned.1.call-start = ((), (), s32[]{:S(2)}) async-start(), calls=%async_computation.13 | async-start | bytes 1327104 | tf_op jit(solution)/shard_map/all_gather | solution.py:176
  219.8 67.5 %all-gather.11.cloned.1.call-start = ((), (), s32[]{:S(2)}) async-start(), calls=%async_computation.12 | async-start | bytes 1966080 | tf_op jit(solution)/shard_map/all_gather | solution.py:205
  253.6 75.8 %all-gather.15.cloned.1.call-start = ((), (), s32[]{:S(2)}) async-start(), calls=%async_computation.14 | async-start | bytes 1327104 | tf_op jit(solution)/shard_map/all_gather | solution.py:178
  254.1 95.5 %all-gather.17.cloned.1.call-start = ((), (), s32[]{:S(2)}) async-start(), calls=%async_computation.16 | async-start | bytes 1966080 | tf_op jit(solution)/shard_map/all_gather | solution.py:215
  257.1 130.1 %reduce-scatter.20.cloned.1.call-start = ((), (), s32[]{:S(2)}) async-start(), calls=%async_computation.17 | async-start | bytes 1966080 | tf_op jit(solution)/shard_map/reduce_scatter | solution.py:224
  358.9 58.9 %reduce-scatter.18.cloned.1.call-start = ((), (), s32[]{:S(2)}) async-start(), calls=%async_computation.15 | async-start | bytes 1966080 | tf_op jit(solution)/shard_map/reduce_scatter | solution.py:210
  363.3 79.1 %all-gather.19.cloned.1.call-start = ((), (), s32[]{:S(2)}) async-start(), calls=%async_computation.18 | async-start | bytes 1966080 | tf_op jit(solution)/shard_map/all_gather | solution.py:233
  422.8 141.6 %reduce-scatter.22.cloned.1.call-start = ((), (), s32[]{:S(2)}) async-start(), calls=%async_computation.19 | async-start | bytes 1966080 | tf_op jit(solution)/shard_map/reduce_scatter | solution.py:258
  502.4 107.0 %reduce-scatter.32.cloned.1.call-start = ((), (), s32[]{:S(2)}) async-start(), calls=%async_computation.24 | async-start | bytes 2654208 | tf_op jit(solution)/shard_map/reduce_scatter | solution.py:284
  507.3 168.4 %reduce-scatter.34.cloned.1.call-start = ((), (), s32[]{:S(2)}) async-start(), calls=%async_computation.25 | async-start | bytes 2654208
  515.3 225.8 %reduce-scatter.30.cloned.1.call-start = ((), (), s32[]{:S(2)}) async-start(), calls=%async_computation.23 | async-start | bytes 884736 | tf_op jit(solution)/shard_map/reduce_scatter | solution.py:283
  518.5 288.4 %reduce-scatter.28.cloned.1.call-start = ((), (), s32[]{:S(2)}) async-start(), calls=%async_computation.22 | async-start | bytes 884736 | tf_op jit(solution)/shard_map/reduce_scatter | solution.py:281
  520.1 352.2 %reduce-scatter.26.cloned.1.call-start = ((), (), s32[]{:S(2)}) async-start(), calls=%async_computation.21 | async-start | bytes 884736 | tf_op jit(solution)/shard_map/reduce_scatter | solution.py:280
  521.8 416.3 %reduce-scatter.24.cloned.1.call-start = ((), (), s32[]{:S(2)}) async-start(), calls=%async_computation.20 | async-start | bytes 884736 | tf_op jit(solution)/shard_map/reduce_scatter | solution.py:278
  (34 other events, 1401.6 us)
Sparse Core Ops, SparseCore 0:
  60.9 16.9 all-gather.8
  219.3 30.2 reduce-scatter.15
  359.0 28.1 reduce-scatter.19
  389.6 28.1 reduce-scatter.17
Sparse Core Ops, SparseCore 1:
  222.1 43.3 all-gather.12
  267.5 18.0 all-gather.10
  287.8 41.5 all-gather.14
  331.6 18.0 all-gather.16
  422.9 19.5 all-gather.18
  502.5 28.1 reduce-scatter.21
  534.6 68.9 reduce-scatter.31
  607.5 68.0 reduce-scatter.33
  679.4 61.6 reduce-scatter.29
  745.3 61.5 reduce-scatter.27
  810.6 61.6 reduce-scatter.25
  876.5 61.5 reduce-scatter.23
